TPU v7x, 32 devices: a whole 2x2x4 slice. The times are simulated.
32 devices in a mesh: row: 2 (over x), col: 4 (over z), freq: 4 (over y, core).
Axes of the slice: x: 2, y: 2, z: 4, core: 2. Of those that a mesh axis runs over, the one named last changes fastest.
Arguments:
- traces: bfloat16 [24, 1024, 512], P(None, ('row', 'col'))
Outputs:
- correlation: float32 [1024, 2, 4, 128], P(('row', 'freq'), None, 'col')
All inputs are finite; a program needn't handle non-finite values.
Results may differ from a plain program's by a relative error of at most 0.0025.
Values may be sent and summed in bfloat16 or wider, within the bound.
A program may use at most 64 MiB of HBM per device.

v0:
```python
import math

import jax
import jax.numpy as jnp
from jax import lax
from jax.sharding import PartitionSpec as P


def spectra_table(samples, bins_local, band):
    times = jnp.arange(samples, dtype=jnp.int32)[:, None]
    bins = band * bins_local + 1 + jnp.arange(bins_local, dtype=jnp.int32)[None, :]
    angle = (times * bins % samples).astype(jnp.float32) * (2.0 * math.pi / samples)
    return jnp.concatenate([jnp.cos(angle), -jnp.sin(angle)], axis=1)


def reduce_bands(partial_tile):
    return lax.psum_scatter(partial_tile, "freq", scatter_dimension=0, tiled=True)


def on_device(traces):
    windows, channels, samples = traces.shape
    bands = lax.axis_size("freq")
    bins_local = samples // 2 // bands
    table = spectra_table(samples, bins_local, lax.axis_index("freq"))
    table_high = table.astype(jnp.bfloat16)
    table_low = (table - table_high.astype(jnp.float32)).astype(jnp.bfloat16)
    both_tables = jnp.concatenate([table_high, table_low], axis=1)
    flat_traces = traces.reshape(windows * channels, samples)
    both_parts = jnp.dot(flat_traces, both_tables, preferred_element_type=jnp.float32)
    spectrum = both_parts[:, : 2 * bins_local] + both_parts[:, 2 * bins_local :]
    spectrum = spectrum.reshape(windows, channels, 2 * bins_local)
    signal = traces.astype(jnp.float32)
    squares = jnp.sum(signal * signal, axis=2)
    alternate = jnp.where(jnp.arange(samples) % 2 == 0, 1.0, -1.0).astype(jnp.float32)
    lowest = jnp.sum(signal, axis=2)
    highest = jnp.sum(signal * alternate[None, None, :], axis=2)
    energy = 0.5 * jnp.sum(samples * squares - lowest * lowest + highest * highest, axis=0)
    inverse = lax.rsqrt(energy / (windows * samples) + 1e-05)
    whitened = (spectrum * inverse[None, :, None]).astype(jnp.bfloat16)
    columns = lax.all_gather(whitened[None], "row", axis=0, tiled=True)
    factor = 1.0 / math.sqrt(windows * samples)
    gathered = lax.all_gather(whitened, "col", axis=1, tiled=True)
    product = jnp.einsum("wak,rwbk->arb", gathered, columns, preferred_element_type=jnp.float32)
    partial_tile = product * factor
    return reduce_bands(partial_tile[:, :, None, :])


def solution(mesh):
    placed = (P(None, ("row", "col"), None),)
    return jax.shard_map(
        on_device,
        mesh=mesh,
        in_specs=placed,
        out_specs=P(("row", "freq"), None, "col", None),
        check_vma=False,
    )
```

profile of v0, /device:TPU:0, one launch (start us, length us, event | category | flops | bytes accessed | tf_op | source)
XLA Modules:
  0.0 142.2 jit_solution(5487202693401866076)
XLA Ops:
  6.5 0.0 copy-start
  6.5 0.0 all-gather.5.cloned.1.call-start
  6.5 1.1 fusion.22
  7.6 0.1 subtract_convert_fusion
  7.7 0.1 fusion.23
  7.9 3.4 %fusion = (f32[24,128]{1,0:T(8,128)S(1)}, f32[24,128]{1,0:T(8,128)S(1)}, f32[24,128]{1,0:T(8,128)S(1)}) fusion(bf16[24,128,512]{2,1,0:T(8,128)(2,1)} %param.1, f32[512]{0:T(512)S(1)} %fusion.27), kind=kLoop, calls=%fused_computation.3 | loop fusion | flops 9427968 | bytes 3184640 | tf_op jit(solution)/shard_map/reduce_sum | solution.py:33
  11.3 0.0 copy-done
  11.3 1.0 convolution_bitcast_fusion
  12.4 0.2 slice_add_fusion
  12.5 0.5 copy.12
  13.0 1.2 multiply_convert_fusion
  14.2 0.0 all-gather.5.cloned.1.call-update
  14.2 0.0 all-gather.3.cloned.1.call-start
  14.3 1.2 multiply_convert_fusion.1
  15.5 0.0 all-gather.3.cloned.1.call-update
  15.5 0.0 reduce-scatter.2.cloned.1.call-start
  15.5 28.7 %all-gather.5.cloned.1.call-done = bf16[2,24,128,128]{3,2,1,0:T(8,128)(2,1)} async-done(((bf16[1,24,128,128]{3,2,1,0:T(8,128)(2,1)}), bf16[2,24,128,128]{3,2,1,0:T(8,128)(2,1)}) %all-gather.5.cloned.1.call-update) | async-done | bytes 1572880 | tf_op jit(solution)/shard_map/all_gather | solution.py:40
  44.3 65.1 %all-gather.3.cloned.1.call-done = bf16[24,512,128]{2,1,0:T(8,128)(2,1)} async-done(((bf16[24,128,128]{2,1,0:T(8,128)(2,1)}), bf16[24,512,128]{2,1,0:T(8,128)(2,1)}) %all-gather.3.cloned.1.call-update) | async-done | bytes 3145744 | tf_op jit(solution)/shard_map/all_gather | solution.py:42
  109.3 4.2 %fusion.10 = f32[512,2,1,128]{3,0,1,2:T(8,128)} fusion(bf16[2,24,128,128]{3,2,1,0:T(8,128)(2,1)} %all-gather.5.cloned.1.call-done, bf16[24,512,128]{2,1,0:T(8,128)(2,1)} %all-gather.3.cloned.1.call-done), kind=kOutput, calls=%fused_computation.13 | convolution fusion | flops 805437440 | bytes 5242880 | tf_op jit(solution)/shard_map/wak,rwbk->arb/dot_general | solution.py:43
  113.5 0.0 reduce-scatter.2.cloned.1.call-update
  113.5 20.5 %reduce-scatter.2.cloned.1.call-done = f32[128,2,1,128]{3,0,1,2:T(8,128)} async-done(((f32[512,2,1,128]{3,0,1,2:T(8,128)}), f32[128,2,1,128]{3,0,1,2:T(8,128)}) %reduce-scatter.2.cloned.1.call-update) | async-done | bytes 131088 | tf_op jit(solution)/shard_map/reduce_scatter | solution.py:17
  134.0 1.7 %copy.10 = f32[128,2,1,128]{3,2,1,0:T(1,128)} copy(f32[128,2,1,128]{3,0,1,2:T(8,128)} %reduce-scatter.2.cloned.1.call-done) | data formatting | bytes 262144 | tf_op jit(solution)/shard_map/reduce_scatter | solution.py:17
  (4 shorter events, 0.0 us)
Async XLA Ops:
  6.5 4.8 %copy-start = (bf16[24,128,512]{2,1,0:T(8,128)(2,1)S(1)}, bf16[24,128,512]{2,1,0:T(8,128)(2,1)}, u32[]{:S(2)}) copy-start(bf16[24,128,512]{2,1,0:T(8,128)(2,1)} %param.1) | copy-start | bytes 9437188
  6.5 37.7 %all-gather.5.cloned.1.call-start = ((), (), s32[]{:S(2)}) async-start(), calls=%async_computation.2 | async-start | bytes 2359296 | tf_op jit(solution)/shard_map/all_gather | solution.py:40
  14.2 95.1 %all-gather.3.cloned.1.call-start = ((), (), s32[]{:S(2)}) async-start(), calls=%async_computation.1 | async-start | bytes 3932160 | tf_op jit(solution)/shard_map/all_gather | solution.py:42
  15.5 118.5 %reduce-scatter.2.cloned.1.call-start = ((), (), s32[]{:S(2)}) async-start(), calls=%async_computation.3 | async-start | bytes 655360 | tf_op jit(solution)/shard_map/reduce_scatter | solution.py:17
Sparse Core Ops, SparseCore 0:
  14.3 29.8 all-gather.4
  45.8 63.4 all-gather.2
  113.7 20.3 reduce-scatter.1
where the time goes:
time: 142 us
  waiting for transfers between devices  114 us (80%)
  between operations  13.2 us (9%)
  other arithmetic  7.3 us (5%)
  matrix products  5.2 us (4%)
  local copies, waits for them, and re-layouts  2.16 us (2%)
    all_gather x1, waiting for transfers between devices, on_device(): gathered = lax.all_gather(whitened, 'col', axis=1, tiled=True)  65.1 us
    all_gather x1, waiting for transfers between devices, on_device(): columns = lax.all_gather(whitened[None], 'row', axis=0, tiled=True)  28.7 us
    reduce_scatter x1, waiting for transfers between devices, reduce_bands(): lax.psum_scatter(partial_tile, 'freq', scatter_dimension=0, tiled=True)  20.5 us
    dot_general x1, matrix products, on_device(): jnp.einsum('wak,rwbk->arb', gathered, columns, preferred_element_type=jnp...  4.18 us
    reduce_sum x1, other arithmetic, on_device(): squares = jnp.sum(signal * signal, axis=2)  3.42 us
  transfers between devices with their start and end apart: 3, of which 3 were waited for; matrix products, arithmetic and copies ran while one was open for 1% of the time, Pallas kernels for 0%

commit v1 on v0

v1 whole, which is shorter than its diff:
```python
import functools
import math

import jax
import jax.numpy as jnp
from jax import lax
from jax.experimental import pallas as pl
from jax.experimental.pallas import tpu as pltpu
from jax.sharding import PartitionSpec as P

MESH = pl.DeviceIdType.MESH
NT = (((1,), (1,)), ((), ()))


def kernel(
    n_row, n_col, n_freq, traces, out, spectra, blocks, whole, send_a, keep_a, recv_a, send_b, keep_b,
    recv_b, send_c, keep_c, recv_c, z_send, z_recv, x_send, x_recv, a_send, a_recv, b_send, b_recv,
    c_send, c_recv,
):
    windows, channels, samples = traces.shape
    part = samples // n_freq
    share = windows // n_col
    rows = n_col * channels // n_freq
    i, j, f = lax.axis_index("row"), lax.axis_index("col"), lax.axis_index("freq")
    core = lax.rem(f, 2)
    side = lax.div(f, 2)
    core_peer = (i, j, f + 1 - 2 * core)
    side_peer = (i, j, lax.rem(f + 2, n_freq))

    def col_peer(d):
        return (i, lax.rem(j + d, n_col), f)

    def row_peer(e):
        return (lax.rem(i + e, n_row), j, f)

    peers = [core_peer, side_peer]
    peers += [col_peer(d) for d in range(1, n_col)]
    peers += [row_peer(e) for e in range(1, n_row)]
    barrier = pltpu.get_barrier_semaphore()
    for peer in peers:
        pl.semaphore_signal(barrier, inc=1, device_id=peer, device_id_type=MESH)

    time = lax.broadcasted_iota(jnp.int32, (samples, 2 * part), 0)
    lane = lax.broadcasted_iota(jnp.int32, (samples, 2 * part), 1)
    odd = jnp.logical_and(lane >= part, lax.rem(time + lane, 2) == 1)
    table = jnp.where(odd, -1.0 / samples, 1.0 / samples).astype(jnp.bfloat16)
    root = math.sqrt(2.0) - 1.0

    def window(w, total):
        record = traces[w]
        parts = jnp.dot(record, table, preferred_element_type=jnp.float32)
        mean, alternate = parts[:, :part], parts[:, part:]
        for q in range(n_freq):
            rest = record[:, q * part : (q + 1) * part].astype(jnp.float32) - mean
            total = total + rest * rest
        total = total + n_freq * alternate * alternate
        own = traces[w, :, pl.ds(pl.multiple_of(f * part, part), part)].astype(jnp.float32)
        spectra[w] = own - mean + root * alternate
        return total

    total = lax.fori_loop(0, windows, window, jnp.zeros((channels, part), jnp.float32))
    energy = (0.5 * samples) * jnp.sum(total, axis=1, keepdims=True)
    inverse = lax.rsqrt(energy / (windows * samples) + 1e-05)

    pl.semaphore_wait(barrier, len(peers))

    def slot(row, col):
        return whole.at[row, pl.ds(pl.multiple_of(col * channels, channels), channels)]

    def forward(d):
        source = slot(i, lax.rem(j + n_col - d, n_col))
        copies = []
        for e in range(1, n_row):
            copy = pltpu.make_async_remote_copy(
                src_ref=source,
                dst_ref=source,
                send_sem=x_send.at[d, e - 1],
                recv_sem=x_recv.at[d, e - 1],
                device_id=row_peer(e),
                device_id_type=MESH,
            )
            copy.start()
            copies.append(copy)
        return copies

    z_copies, x_copies = [], []
    for d in range(n_col):
        target = lax.rem(j + d, n_col)
        for k in range(share):
            white = (spectra[target * share + k] * inverse).astype(jnp.bfloat16)
            if d == 0:
                whole[i, pl.ds(pl.multiple_of(j * channels, channels), channels), pl.ds(k * part, part)] = white
            else:
                blocks[d - 1, :, pl.ds(k * part, part)] = white
        if d == 0:
            x_copies += forward(0)
        else:
            copy = pltpu.make_async_remote_copy(
                src_ref=blocks.at[d - 1],
                dst_ref=slot(i, j),
                send_sem=z_send.at[d - 1],
                recv_sem=z_recv.at[d - 1],
                device_id=col_peer(d),
                device_id_type=MESH,
            )
            copy.start()
            z_copies.append(copy)
    nearest = sorted(range(1, n_col), key=lambda d: (min(d, n_col - d), d))
    for d in nearest:
        z_copies[d - 1].wait_recv()
        x_copies += forward(d)
    for copy in x_copies:
        copy.wait_recv()

    width = n_row * channels

    def own_rows(c):
        picked = []
        for s in range(n_freq // 2):
            first = (2 * s + c) * rows
            picked.append(whole[i, pl.ds(pl.multiple_of(first, rows), rows), :])
        return jnp.concatenate(picked, axis=0)

    a_copies, b_copies, c_copies = [], [], []
    order = list(range(1, n_col)) + [0]

    def stage_a(t):
        target = lax.rem(j + order[t], n_col)
        columns = jnp.concatenate(
            [whole[r, pl.ds(pl.multiple_of(target * channels, channels), channels), :] for r in range(n_row)],
            axis=0,
        )
        away = lax.dot_general(own_rows(1 - core), columns, NT, preferred_element_type=jnp.float32)
        send_a[t] = away.astype(jnp.bfloat16).reshape(2, rows, width)
        copy = pltpu.make_async_remote_copy(
            src_ref=send_a.at[t],
            dst_ref=recv_a.at[t],
            send_sem=a_send.at[t],
            recv_sem=a_recv.at[t],
            device_id=core_peer,
            device_id_type=MESH,
        )
        copy.start()
        a_copies.append(copy)
        near = lax.dot_general(own_rows(core), columns, NT, preferred_element_type=jnp.float32)
        keep_a[t % 2] = near.reshape(2, rows, width)

    def stage_b(t):
        a_copies[t].wait_recv()
        away = keep_a[t % 2, 1 - side] + recv_a[t, 1 - side].astype(jnp.float32)
        send_b[t] = away.astype(jnp.bfloat16)
        copy = pltpu.make_async_remote_copy(
            src_ref=send_b.at[t],
            dst_ref=recv_b.at[t],
            send_sem=b_send.at[t],
            recv_sem=b_recv.at[t],
            device_id=side_peer,
            device_id_type=MESH,
        )
        copy.start()
        b_copies.append(copy)
        keep_b[t % 2] = keep_a[t % 2, side] + recv_a[t, side].astype(jnp.float32)

    def stage_c(t):
        d = order[t]
        b_copies[t].wait_recv()
        value = keep_b[t % 2] + recv_b[t].astype(jnp.float32)
        if d == 0:
            keep_c[...] = value
            return
        send_c[d - 1] = value.astype(jnp.bfloat16)
        copy = pltpu.make_async_remote_copy(
            src_ref=send_c.at[d - 1],
            dst_ref=recv_c.at[d - 1],
            send_sem=c_send.at[d - 1],
            recv_sem=c_recv.at[d - 1],
            device_id=col_peer(d),
            device_id_type=MESH,
        )
        copy.start()
        c_copies.append(copy)

    for t in range(n_col + 2):
        if t < n_col:
            stage_a(t)
        if 1 <= t <= n_col:
            stage_b(t - 1)
        if t >= 2:
            stage_c(t - 2)

    value = keep_c[...]
    for d in range(1, n_col):
        c_copies[d - 1].wait_recv()
        value = value + recv_c[d - 1].astype(jnp.float32)
    value = value * (0.5 * samples / math.sqrt(windows * samples))
    for r in range(n_row):
        out[:, r, 0, :] = value[:, r * channels : (r + 1) * channels]
    for copy in z_copies + x_copies + a_copies + b_copies + c_copies:
        copy.wait_send()


def on_device(n_row, n_col, n_freq, traces):
    windows, channels, samples = traces.shape
    part = samples // n_freq
    depth = windows // n_col * part
    rows = n_col * channels // n_freq
    width = n_row * channels
    bf16, f32, dma = jnp.bfloat16, jnp.float32, pltpu.SemaphoreType.DMA
    return pl.pallas_call(
        functools.partial(kernel, n_row, n_col, n_freq),
        out_shape=jax.ShapeDtypeStruct((rows, n_row, 1, channels), f32),
        in_specs=[pl.BlockSpec(memory_space=pltpu.VMEM)],
        out_specs=pl.BlockSpec(memory_space=pltpu.VMEM),
        scratch_shapes=[
            pltpu.VMEM((windows, channels, part), f32),
            pltpu.VMEM((n_col - 1, channels, depth), bf16),
            pltpu.VMEM((n_row, n_col * channels, depth), bf16),
            pltpu.VMEM((n_col, 2, rows, width), bf16),
            pltpu.VMEM((2, 2, rows, width), f32),
            pltpu.VMEM((n_col, 2, rows, width), bf16),
            pltpu.VMEM((n_col, rows, width), bf16),
            pltpu.VMEM((2, rows, width), f32),
            pltpu.VMEM((n_col, rows, width), bf16),
            pltpu.VMEM((n_col - 1, rows, width), bf16),
            pltpu.VMEM((rows, width), f32),
            pltpu.VMEM((n_col - 1, rows, width), bf16),
            dma((n_col - 1,)),
            dma((n_col - 1,)),
            dma((n_col, n_row - 1)),
            dma((n_col, n_row - 1)),
            dma((n_col,)),
            dma((n_col,)),
            dma((n_col,)),
            dma((n_col,)),
            dma((n_col - 1,)),
            dma((n_col - 1,)),
        ],
        compiler_params=pltpu.CompilerParams(
            collective_id=0, has_side_effects=True, vmem_limit_bytes=56 * 1024 * 1024
        ),
    )(traces)


def solution(mesh):
    sizes = [mesh.shape[axis] for axis in ("row", "col", "freq")]
    return jax.shard_map(
        functools.partial(on_device, *sizes),
        mesh=mesh,
        in_specs=(P(None, ("row", "col"), None),),
        out_specs=P(("row", "freq"), None, "col", None),
        check_vma=False,
    )
```

time: 142 us -> 54.1 us (0.38)
  waiting for transfers between devices: 114 us -> 0 us
  Pallas kernels: 0 us -> 52.3 us
  between operations: 13.2 us -> 0.01 us
  other arithmetic: 7.3 us -> 0 us
  matrix products: 5.2 us -> 0 us
    all_gather x2 -> x0, waiting for transfers between devices: 93.8 us -> none  [the longest x1 65.1 us: on_device(): gathered = lax.all_gather(whitened, 'col', axis=1, tiled=True)]
    pallas_call x0 -> x1, Pallas kernels: none -> 52.3 us  [on_device(): pl.pallas_call(functools.partial(kernel, n_row, n_col, n_freq), out_shape...]
    reduce_scatter x1 -> x0, waiting for transfers between devices: 20.5 us -> none  [reduce_bands(): lax.psum_scatter(partial_tile, 'freq', scatter_dimension=0, tiled=True)]
    dot_general x2 -> x0, matrix products: 5.2 us -> none  [the longest x1 4.18 us: on_device(): jnp.einsum('wak,rwbk->arb', gathered, columns, preferred_element_type=jnp...]
    reduce_sum x2 -> x0, other arithmetic: 3.45 us -> none  [the longest x1 3.42 us: on_device(): squares = jnp.sum(signal * signal, axis=2)]
    convert_element_type x4 -> x0, other arithmetic: 2.61 us -> none  [the longest x2 2.37 us: on_device(): whitened = (spectrum * inverse[None, :, None]).astype(jnp.bfloat16)]
    reduce_scatter x1 -> x0, local copies, waits for them, and re-layouts: 1.69 us -> none  [reduce_bands(): lax.psum_scatter(partial_tile, 'freq', scatter_dimension=0, tiled=True)]
    unnamed x2 -> x1, local copies, waits for them, and re-layouts: 0.01 us -> 1.57 us
  transfers between devices with their start and end apart: 3 -> 0, of which waited for: 3 -> 0; matrix products, arithmetic and copies ran while one was open for 1% -> 0% of each run, Pallas kernels for 0% -> 0%
where the time goes in v1:
time: 54.1 us; the launch traced here: 53.9 us
  Pallas kernels  52.3 us (97%)
  local copies, waits for them, and re-layouts  1.57 us (3%)
    pallas_call x1, Pallas kernels, on_device(): pl.pallas_call(functools.partial(kernel, n_row, n_col, n_freq), out_shape...  52.3 us
    unnamed x1, local copies, waits for them, and re-layouts  1.57 us

profile of v1, /device:TPU:0, one launch (start us, length us, event | category | flops | bytes accessed | tf_op | source)
XLA Modules:
  0.0 53.9 jit_solution(12727342833598293710)
XLA Ops:
  0.0 52.3 %shard_map.17 = f32[128,2,1,128]{3,2,1,0:T(1,128)} custom-call(bf16[24,128,512]{2,1,0:T(8,128)(2,1)} %traces.1), custom_call_target="tpu_custom_call" | custom-call | tf_op jit(solution)/shard_map/pallas_call | solution.py:209
  52.4 1.6 %copy.3 = f32[128,2,1,128]{3,2,1,0:T(1,128)} copy(f32[128,2,1,128]{3,2,1,0:T(1,128)} %shard_map.17) | data formatting | bytes 262144

commit v2 on v1

v2 whole, which is shorter than its diff:
```python
import functools
import math

import jax
import jax.numpy as jnp
from jax import lax
from jax.experimental import pallas as pl
from jax.experimental.pallas import tpu as pltpu
from jax.sharding import PartitionSpec as P

MESH = pl.DeviceIdType.MESH
NT = (((1,), (1,)), ((), ()))


def kernel(
    n_row, n_col, n_freq, given, out, traces, spectra, blocks, whole,
    send_a0, keep_a0, recv_a0, send_b0, keep_b0, recv_b0, send_c0, keep_c0, recv_c0,
    send_a1, keep_a1, recv_a1, send_b1, keep_b1, recv_b1, send_c1, keep_c1, recv_c1,
    z_send, z_recv, x_send, x_recv, a_send, a_recv, b_send, b_recv, c_send, c_recv, load,
):
    groups = (
        (send_a0, keep_a0, recv_a0, send_b0, keep_b0, recv_b0, send_c0, keep_c0, recv_c0),
        (send_a1, keep_a1, recv_a1, send_b1, keep_b1, recv_b1, send_c1, keep_c1, recv_c1),
    )
    windows, channels, samples = traces.shape
    part = samples // n_freq
    share = windows // n_col
    rows = n_col * channels // n_freq
    i, j, f = lax.axis_index("row"), lax.axis_index("col"), lax.axis_index("freq")
    core = lax.rem(f, 2)
    side = lax.div(f, 2)
    core_peer = (i, j, f + 1 - 2 * core)
    side_peer = (i, j, lax.rem(f + 2, n_freq))

    def col_peer(d):
        return (i, lax.rem(j + d, n_col), f)

    def row_peer(e):
        return (lax.rem(i + e, n_row), j, f)

    peers = [core_peer, side_peer]
    peers += [col_peer(d) for d in range(1, n_col)]
    peers += [row_peer(e) for e in range(1, n_row)]
    barrier = pltpu.get_barrier_semaphore()
    for peer in peers:
        pl.semaphore_signal(barrier, inc=1, device_id=peer, device_id_type=MESH)

    loads = []
    batch = windows // n_col
    for p in range(n_col):
        group = pl.ds(p * batch, batch)
        copy = pltpu.make_async_copy(given.at[group], traces.at[group], load.at[p])
        copy.start()
        loads.append(copy)

    time = lax.broadcasted_iota(jnp.int32, (samples, 2 * part), 0)
    lane = lax.broadcasted_iota(jnp.int32, (samples, 2 * part), 1)
    odd = jnp.logical_and(lane >= part, lax.rem(time + lane, 2) == 1)
    table = jnp.where(odd, -1.0 / samples, 1.0 / samples).astype(jnp.bfloat16)
    root = math.sqrt(2.0) - 1.0

    def window(w, total):
        record = traces[w]
        parts = jnp.dot(record, table, preferred_element_type=jnp.float32)
        mean, alternate = parts[:, :part], parts[:, part:]
        for q in range(n_freq):
            rest = record[:, q * part : (q + 1) * part].astype(jnp.float32) - mean
            total = total + rest * rest
        total = total + n_freq * alternate * alternate
        own = traces[w, :, pl.ds(pl.multiple_of(f * part, part), part)].astype(jnp.float32)
        spectra[w] = own - mean + root * alternate
        return total

    total = jnp.zeros((channels, part), jnp.float32)
    for p in range(n_col):
        loads[p].wait()
        total = lax.fori_loop(p * batch, (p + 1) * batch, window, total)
    energy = (0.5 * samples) * jnp.sum(total, axis=1, keepdims=True)
    inverse = lax.rsqrt(energy / (windows * samples) + 1e-05)

    pl.semaphore_wait(barrier, len(peers))

    chunks = math.gcd(share, 3)
    span = share // chunks * part

    def slot(row, col, c):
        return whole.at[
            row, pl.ds(pl.multiple_of(col * channels, channels), channels), pl.ds(c * span, span)
        ]

    def forward(d, c):
        source = slot(i, lax.rem(j + n_col - d, n_col), c)
        copies = []
        for e in range(1, n_row):
            copy = pltpu.make_async_remote_copy(
                src_ref=source,
                dst_ref=source,
                send_sem=x_send.at[c, d, e - 1],
                recv_sem=x_recv.at[c, d, e - 1],
                device_id=row_peer(e),
                device_id_type=MESH,
            )
            copy.start()
            copies.append(copy)
        return copies

    z_copies, x_copies = {}, []
    for c in range(chunks):
        for d in range(n_col):
            target = lax.rem(j + d, n_col)
            for k in range(c * share // chunks, (c + 1) * share // chunks):
                white = (spectra[target * share + k] * inverse).astype(jnp.bfloat16)
                lanes = pl.ds(k * part, part)
                if d == 0:
                    whole[i, pl.ds(pl.multiple_of(j * channels, channels), channels), lanes] = white
                else:
                    blocks[d - 1, :, lanes] = white
            if d == 0:
                x_copies += forward(0, c)
            else:
                copy = pltpu.make_async_remote_copy(
                    src_ref=blocks.at[d - 1, :, pl.ds(c * span, span)],
                    dst_ref=slot(i, j, c),
                    send_sem=z_send.at[c, d - 1],
                    recv_sem=z_recv.at[c, d - 1],
                    device_id=col_peer(d),
                    device_id_type=MESH,
                )
                copy.start()
                z_copies[c, d] = copy
    nearest = sorted(range(1, n_col), key=lambda d: (min(d, n_col - d), d))
    for c in range(chunks):
        for d in nearest:
            z_copies[c, d].wait_recv()
            x_copies += forward(d, c)
    z_copies = list(z_copies.values())

    def own_rows(c):
        picked = []
        for s in range(n_freq // 2):
            first = (2 * s + c) * rows
            picked.append(whole[i, pl.ds(pl.multiple_of(first, rows), rows), :])
        return jnp.concatenate(picked, axis=0)

    out_copies = []
    order = list(range(1, n_col)) + [0]

    def remote(source, target, send, receive, peer):
        copy = pltpu.make_async_remote_copy(
            src_ref=source,
            dst_ref=target,
            send_sem=send,
            recv_sem=receive,
            device_id=peer,
            device_id_type=MESH,
        )
        copy.start()
        out_copies.append(copy)
        return copy

    def run(g, t, stage):
        shifts = [0] if g == 0 else list(range(1, n_row))
        wide = len(shifts) * channels
        send_a, keep_a, recv_a, send_b, keep_b, recv_b, send_c, keep_c, recv_c = groups[g]
        d = order[t]
        if stage == 0:
            target = pl.ds(pl.multiple_of(lax.rem(j + d, n_col) * channels, channels), channels)
            columns = jnp.concatenate([whole[lax.rem(i + e, n_row), target, :] for e in shifts], axis=0)
            away = lax.dot_general(own_rows(1 - core), columns, NT, preferred_element_type=jnp.float32)
            send_a[t] = away.astype(jnp.bfloat16).reshape(2, rows, wide)
            a_copies[g, t] = remote(
                send_a.at[t], recv_a.at[t], a_send.at[g, t], a_recv.at[g, t], core_peer
            )
            near = lax.dot_general(own_rows(core), columns, NT, preferred_element_type=jnp.float32)
            keep_a[t % 2] = near.reshape(2, rows, wide)
        elif stage == 1:
            a_copies[g, t].wait_recv()
            away = keep_a[t % 2, 1 - side] + recv_a[t, 1 - side].astype(jnp.float32)
            send_b[t] = away.astype(jnp.bfloat16)
            b_copies[g, t] = remote(
                send_b.at[t], recv_b.at[t], b_send.at[g, t], b_recv.at[g, t], side_peer
            )
            keep_b[t % 2] = keep_a[t % 2, side] + recv_a[t, side].astype(jnp.float32)
        else:
            b_copies[g, t].wait_recv()
            value = keep_b[t % 2] + recv_b[t].astype(jnp.float32)
            if d == 0:
                keep_c[...] = value
                return
            send_c[d - 1] = value.astype(jnp.bfloat16)
            c_copies[g, d] = remote(
                send_c.at[d - 1], recv_c.at[d - 1], c_send.at[g, d - 1], c_recv.at[g, d - 1], col_peer(d)
            )

    a_copies, b_copies, c_copies = {}, {}, {}
    for g in range(2):
        if g == 1:
            for copy in x_copies:
                copy.wait_recv()
        for t in range(n_col + 2):
            if t < n_col:
                run(g, t, 0)
            if 1 <= t <= n_col:
                run(g, t - 1, 1)
            if t >= 2:
                run(g, t - 2, 2)

    for g in range(2):
        keep_c, recv_c = groups[g][7:]
        value = keep_c[...]
        for d in range(1, n_col):
            c_copies[g, d].wait_recv()
            value = value + recv_c[d - 1].astype(jnp.float32)
        value = value * (0.5 * samples / math.sqrt(windows * samples))
        for n, e in enumerate([0] if g == 0 else range(1, n_row)):
            place = pl.ds(pl.multiple_of(lax.rem(i + e, n_row) * channels, channels), channels)
            out[:, place] = value[:, n * channels : (n + 1) * channels]
    for copy in z_copies + x_copies + out_copies:
        copy.wait_send()


def on_device(n_row, n_col, n_freq, traces):
    windows, channels, samples = traces.shape
    part = samples // n_freq
    depth = windows // n_col * part
    rows = n_col * channels // n_freq
    chunks = math.gcd(windows // n_col, 3)
    bf16, f32, dma = jnp.bfloat16, jnp.float32, pltpu.SemaphoreType.DMA

    def tiles(width):
        return [
            pltpu.VMEM((n_col, 2, rows, width), bf16),
            pltpu.VMEM((2, 2, rows, width), f32),
            pltpu.VMEM((n_col, 2, rows, width), bf16),
            pltpu.VMEM((n_col, rows, width), bf16),
            pltpu.VMEM((2, rows, width), f32),
            pltpu.VMEM((n_col, rows, width), bf16),
            pltpu.VMEM((n_col - 1, rows, width), bf16),
            pltpu.VMEM((rows, width), f32),
            pltpu.VMEM((n_col - 1, rows, width), bf16),
        ]

    result = pl.pallas_call(
        functools.partial(kernel, n_row, n_col, n_freq),
        out_shape=jax.ShapeDtypeStruct((rows, n_row * channels), f32),
        in_specs=[pl.BlockSpec(memory_space=pl.ANY)],
        out_specs=pl.BlockSpec(memory_space=pltpu.VMEM),
        scratch_shapes=[
            pltpu.VMEM((windows, channels, samples), bf16),
            pltpu.VMEM((windows, channels, part), f32),
            pltpu.VMEM((n_col - 1, channels, depth), bf16),
            pltpu.VMEM((n_row, n_col * channels, depth), bf16),
            *tiles(channels),
            *tiles((n_row - 1) * channels),
            dma((chunks, n_col - 1)),
            dma((chunks, n_col - 1)),
            dma((chunks, n_col, n_row - 1)),
            dma((chunks, n_col, n_row - 1)),
            dma((2, n_col)),
            dma((2, n_col)),
            dma((2, n_col)),
            dma((2, n_col)),
            dma((2, n_col - 1)),
            dma((2, n_col - 1)),
            dma((n_col,)),
        ],
        compiler_params=pltpu.CompilerParams(
            collective_id=0, has_side_effects=True, vmem_limit_bytes=56 * 1024 * 1024
        ),
    )(traces)
    return result.reshape(rows, n_row, 1, channels)


def solution(mesh):
    sizes = [mesh.shape[axis] for axis in ("row", "col", "freq")]
    return jax.shard_map(
        functools.partial(on_device, *sizes),
        mesh=mesh,
        in_specs=(P(None, ("row", "col"), None),),
        out_specs=P(("row", "freq"), None, "col", None),
        check_vma=False,
    )
```

time: 54.1 us -> 50.1 us (0.926)
  Pallas kernels: 52.3 us -> 48.3 us
    pallas_call x1, Pallas kernels: 52.3 us -> 48.3 us  [on_device(): pl.pallas_call(functools.partial(kernel, n_row, n_col, n_freq), out_shape...]
    reshape x0 -> x1, local copies, waits for them, and re-layouts: none -> 1.62 us  [on_device(): return result.reshape(rows, n_row, 1, channels)]
    unnamed x1 -> x0, local copies, waits for them, and re-layouts: 1.57 us -> none
where the time goes in v2:
time: 50.1 us; the launch traced here: 50 us
  Pallas kernels  48.3 us (96%)
  local copies, waits for them, and re-layouts  1.62 us (3%)
    pallas_call x1, Pallas kernels, on_device(): pl.pallas_call(functools.partial(kernel, n_row, n_col, n_freq), out_shape...  48.3 us
    reshape x1, local copies, waits for them, and re-layouts, on_device(): return result.reshape(rows, n_row, 1, channels)  1.62 us

profile of v2, /device:TPU:0, one launch (start us, length us, event | category | flops | bytes accessed | tf_op | source)
XLA Modules:
  0.0 50.0 jit_solution(8773072823472086357)
XLA Ops:
  0.0 48.3 %shard_map.17 = f32[128,256]{1,0:T(8,128)} custom-call(bf16[24,128,512]{2,1,0:T(8,128)(2,1)} %given.1), custom_call_target="tpu_custom_call" | custom-call | tf_op jit(solution)/shard_map/pallas_call | solution.py:243
  48.3 1.6 %reshape.3 = f32[128,2,1,128]{3,1,0,2:T(2,128)} reshape(f32[128,256]{1,0:T(8,128)} %shard_map.17) | data formatting | bytes 262144 | tf_op jit(solution)/shard_map/reshape | solution.py:271

commit v3 on v2

--- a/solution.py
+++ b/solution.py
@@ -172,18 +172,18 @@
                 send_a.at[t], recv_a.at[t], a_send.at[g, t], a_recv.at[g, t], core_peer
             )
             near = lax.dot_general(own_rows(core), columns, NT, preferred_element_type=jnp.float32)
-            keep_a[t % 2] = near.reshape(2, rows, wide)
+            keep_a[t % slots] = near.reshape(2, rows, wide)
         elif stage == 1:
             a_copies[g, t].wait_recv()
-            away = keep_a[t % 2, 1 - side] + recv_a[t, 1 - side].astype(jnp.float32)
+            away = keep_a[t % slots, 1 - side] + recv_a[t, 1 - side].astype(jnp.float32)
             send_b[t] = away.astype(jnp.bfloat16)
             b_copies[g, t] = remote(
                 send_b.at[t], recv_b.at[t], b_send.at[g, t], b_recv.at[g, t], side_peer
             )
-            keep_b[t % 2] = keep_a[t % 2, side] + recv_a[t, side].astype(jnp.float32)
+            keep_b[t % slots] = keep_a[t % slots, side] + recv_a[t, side].astype(jnp.float32)
         else:
             b_copies[g, t].wait_recv()
-            value = keep_b[t % 2] + recv_b[t].astype(jnp.float32)
+            value = keep_b[t % slots] + recv_b[t].astype(jnp.float32)
             if d == 0:
                 keep_c[...] = value
                 return
@@ -192,18 +192,16 @@
                 send_c.at[d - 1], recv_c.at[d - 1], c_send.at[g, d - 1], c_recv.at[g, d - 1], col_peer(d)
             )
 
+    slots = keep_a0.shape[0]
     a_copies, b_copies, c_copies = {}, {}, {}
     for g in range(2):
         if g == 1:
             for copy in x_copies:
                 copy.wait_recv()
-        for t in range(n_col + 2):
-            if t < n_col:
-                run(g, t, 0)
-            if 1 <= t <= n_col:
-                run(g, t - 1, 1)
-            if t >= 2:
-                run(g, t - 2, 2)
+        for t in range(n_col + 2 * slots):
+            for stage in range(3):
+                if 0 <= t - stage * (slots - 1) < n_col:
+                    run(g, t - stage * (slots - 1), stage)
 
     for g in range(2):
         keep_c, recv_c = groups[g][7:]
@@ -225,15 +223,16 @@
     depth = windows // n_col * part
     rows = n_col * channels // n_freq
     chunks = math.gcd(windows // n_col, 3)
+    slots = min(n_col, 4)
     bf16, f32, dma = jnp.bfloat16, jnp.float32, pltpu.SemaphoreType.DMA
 
     def tiles(width):
         return [
             pltpu.VMEM((n_col, 2, rows, width), bf16),
-            pltpu.VMEM((2, 2, rows, width), f32),
+            pltpu.VMEM((slots, 2, rows, width), f32),
             pltpu.VMEM((n_col, 2, rows, width), bf16),
             pltpu.VMEM((n_col, rows, width), bf16),
-            pltpu.VMEM((2, rows, width), f32),
+            pltpu.VMEM((slots, rows, width), f32),
             pltpu.VMEM((n_col, rows, width), bf16),
             pltpu.VMEM((n_col - 1, rows, width), bf16),
             pltpu.VMEM((rows, width), f32),

time: 50.1 us -> 46.3 us (0.924)
  Pallas kernels: 48.3 us -> 44.5 us
    pallas_call x1, Pallas kernels: 48.3 us -> 44.5 us  [on_device(): pl.pallas_call(functools.partial(kernel, n_row, n_col, n_freq), out_shape...]
where the time goes in v3:
time: 46.3 us; the launch traced here: 46.1 us
  Pallas kernels  44.5 us (96%)
  local copies, waits for them, and re-layouts  1.62 us (3%)
    pallas_call x1, Pallas kernels, on_device(): pl.pallas_call(functools.partial(kernel, n_row, n_col, n_freq), out_shape...  44.5 us
    reshape x1, local copies, waits for them, and re-layouts, on_device(): return result.reshape(rows, n_row, 1, channels)  1.62 us

profile of v3, /device:TPU:0, one launch (start us, length us, event | category | flops | bytes accessed | tf_op | source)
XLA Modules:
  0.0 46.1 jit_solution(15887982683075650282)
XLA Ops:
  0.0 44.5 %shard_map.17 = f32[128,256]{1,0:T(8,128)} custom-call(bf16[24,128,512]{2,1,0:T(8,128)(2,1)} %given.1), custom_call_target="tpu_custom_call" | custom-call | tf_op jit(solution)/shard_map/pallas_call | solution.py:242
  44.5 1.6 %reshape.3 = f32[128,2,1,128]{3,1,0,2:T(2,128)} reshape(f32[128,256]{1,0:T(8,128)} %shard_map.17) | data formatting | bytes 262144 | tf_op jit(solution)/shard_map/reshape | solution.py:270

commit v4 on v3

--- a/solution.py
+++ b/solution.py
@@ -104,10 +104,12 @@
             copies.append(copy)
         return copies
 
-    z_copies, x_copies = {}, []
-    for c in range(chunks):
-        for d in range(n_col):
-            target = lax.rem(j + d, n_col)
+    z_copies, x_blocks = {}, {}
+    nearest = sorted(range(1, n_col), key=lambda d: (min(d, n_col - d), d))
+
+    def issue(d):
+        target = lax.rem(j + d, n_col)
+        for c in range(chunks):
             for k in range(c * share // chunks, (c + 1) * share // chunks):
                 white = (spectra[target * share + k] * inverse).astype(jnp.bfloat16)
                 lanes = pl.ds(k * part, part)
@@ -116,23 +118,31 @@
                 else:
                     blocks[d - 1, :, lanes] = white
             if d == 0:
-                x_copies += forward(0, c)
-            else:
-                copy = pltpu.make_async_remote_copy(
-                    src_ref=blocks.at[d - 1, :, pl.ds(c * span, span)],
-                    dst_ref=slot(i, j, c),
-                    send_sem=z_send.at[c, d - 1],
-                    recv_sem=z_recv.at[c, d - 1],
-                    device_id=col_peer(d),
-                    device_id_type=MESH,
-                )
-                copy.start()
-                z_copies[c, d] = copy
-    nearest = sorted(range(1, n_col), key=lambda d: (min(d, n_col - d), d))
-    for c in range(chunks):
-        for d in nearest:
-            z_copies[c, d].wait_recv()
-            x_copies += forward(d, c)
+                x_blocks[0, c] = forward(0, c)
+                continue
+            copy = pltpu.make_async_remote_copy(
+                src_ref=blocks.at[d - 1, :, pl.ds(c * span, span)],
+                dst_ref=slot(i, j, c),
+                send_sem=z_send.at[c, d - 1],
+                recv_sem=z_recv.at[c, d - 1],
+                device_id=col_peer(d),
+                device_id_type=MESH,
+            )
+            copy.start()
+            z_copies[c, d] = copy
+
+    ahead = 2
+    issue(nearest[0])
+    issue(0)
+    for n in range(1, len(nearest) + ahead):
+        if n < len(nearest):
+            issue(nearest[n])
+        if n >= ahead:
+            for c in range(chunks):
+                d = nearest[n - ahead]
+                z_copies[c, d].wait_recv()
+                x_blocks[d, c] = forward(d, c)
+    x_copies = [copy for copies in x_blocks.values() for copy in copies]
     z_copies = list(z_copies.values())
 
     def own_rows(c):
@@ -143,7 +153,7 @@
         return jnp.concatenate(picked, axis=0)
 
     out_copies = []
-    order = list(range(1, n_col)) + [0]
+    orders = [list(range(1, n_col)) + [0], [(n_col - d) % n_col for d in [0] + nearest]]
 
     def remote(source, target, send, receive, peer):
         copy = pltpu.make_async_remote_copy(
@@ -162,8 +172,12 @@
         shifts = [0] if g == 0 else list(range(1, n_row))
         wide = len(shifts) * channels
         send_a, keep_a, recv_a, send_b, keep_b, recv_b, send_c, keep_c, recv_c = groups[g]
-        d = order[t]
+        d = orders[g][t]
         if stage == 0:
+            if g == 1:
+                for c in range(chunks):
+                    for copy in x_blocks[(n_col - d) % n_col, c]:
+                        copy.wait_recv()
             target = pl.ds(pl.multiple_of(lax.rem(j + d, n_col) * channels, channels), channels)
             columns = jnp.concatenate([whole[lax.rem(i + e, n_row), target, :] for e in shifts], axis=0)
             away = lax.dot_general(own_rows(1 - core), columns, NT, preferred_element_type=jnp.float32)
@@ -194,14 +208,26 @@
 
     slots = keep_a0.shape[0]
     a_copies, b_copies, c_copies = {}, {}, {}
-    for g in range(2):
-        if g == 1:
-            for copy in x_copies:
-                copy.wait_recv()
-        for t in range(n_col + 2 * slots):
-            for stage in range(3):
-                if 0 <= t - stage * (slots - 1) < n_col:
-                    run(g, t - stage * (slots - 1), stage)
+    lead = slots - 1
+    plans = [
+        [
+            (g, t - stage * lead, stage)
+            for t in range(n_col + 2 * lead)
+            for stage in range(3)
+            if 0 <= t - stage * lead < n_col
+        ]
+        for g in range(2)
+    ]
+    early, late = plans[0], plans[1]
+    if n_col <= slots:
+        early = [step for step in plans[0] if step[2] < 2]
+        late = [step for step in plans[1] if step[2] == 0]
+        late += [step for step in plans[0] if step[2] == 2]
+        late += [step for step in plans[1] if step[2] > 0]
+    for step in early:
+        run(*step)
+    for step in late:
+        run(*step)
 
     for g in range(2):
         keep_c, recv_c = groups[g][7:]

time: 46.3 us -> 44.7 us (0.965)
  Pallas kernels: 44.5 us -> 43 us
    pallas_call x1, Pallas kernels: 44.5 us -> 43 us  [on_device(): pl.pallas_call(functools.partial(kernel, n_row, n_col, n_freq), out_shape...]
where the time goes in v4:
time: 44.7 us; the launch traced here: 44.6 us
  Pallas kernels  43 us (96%)
  local copies, waits for them, and re-layouts  1.62 us (4%)
    pallas_call x1, Pallas kernels, on_device(): pl.pallas_call(functools.partial(kernel, n_row, n_col, n_freq), out_shape...  43 us
    reshape x1, local copies, waits for them, and re-layouts, on_device(): return result.reshape(rows, n_row, 1, channels)  1.62 us

profile of v4, /device:TPU:0, one launch (start us, length us, event | category | flops | bytes accessed | tf_op | source)
XLA Modules:
  0.0 44.6 jit_solution(7762936793184747445)
XLA Ops:
  0.0 43.0 %shard_map.17 = f32[128,256]{1,0:T(8,128)} custom-call(bf16[24,128,512]{2,1,0:T(8,128)(2,1)} %given.1), custom_call_target="tpu_custom_call" | custom-call | tf_op jit(solution)/shard_map/pallas_call | solution.py:268
  43.0 1.6 %reshape.3 = f32[128,2,1,128]{3,1,0,2:T(2,128)} reshape(f32[128,256]{1,0:T(8,128)} %shard_map.17) | data formatting | bytes 262144 | tf_op jit(solution)/shard_map/reshape | solution.py:296

commit v5 on v4

--- a/solution.py
+++ b/solution.py
@@ -74,7 +74,7 @@
     total = jnp.zeros((channels, part), jnp.float32)
     for p in range(n_col):
         loads[p].wait()
-        total = lax.fori_loop(p * batch, (p + 1) * batch, window, total)
+        total = lax.fori_loop(p * batch, (p + 1) * batch, window, total, unroll=True)
     energy = (0.5 * samples) * jnp.sum(total, axis=1, keepdims=True)
     inverse = lax.rsqrt(energy / (windows * samples) + 1e-05)
 

time: 44.7 us -> 41.7 us (0.933)
  Pallas kernels: 43 us -> 39.9 us
    pallas_call x1, Pallas kernels: 43 us -> 39.9 us  [on_device(): pl.pallas_call(functools.partial(kernel, n_row, n_col, n_freq), out_shape...]
where the time goes in v5:
time: 41.7 us; the launch traced here: 41.6 us
  Pallas kernels  39.9 us (96%)
  local copies, waits for them, and re-layouts  1.62 us (4%)
    pallas_call x1, Pallas kernels, on_device(): pl.pallas_call(functools.partial(kernel, n_row, n_col, n_freq), out_shape...  39.9 us
    reshape x1, local copies, waits for them, and re-layouts, on_device(): return result.reshape(rows, n_row, 1, channels)  1.62 us

profile of v5, /device:TPU:0, one launch (start us, length us, event | category | flops | bytes accessed | tf_op | source)
XLA Modules:
  0.0 41.6 jit_solution(15040180405447583691)
XLA Ops:
  0.0 39.9 %shard_map.17 = f32[128,256]{1,0:T(8,128)} custom-call(bf16[24,128,512]{2,1,0:T(8,128)(2,1)} %given.1), custom_call_target="tpu_custom_call" | custom-call | tf_op jit(solution)/shard_map/pallas_call | solution.py:268
  39.9 1.6 %reshape.3 = f32[128,2,1,128]{3,1,0,2:T(2,128)} reshape(f32[128,256]{1,0:T(8,128)} %shard_map.17) | data formatting | bytes 262144 | tf_op jit(solution)/shard_map/reshape | solution.py:296
